TPU v7x, 32 devices: a whole 2x2x4 slice. The times are simulated.
32 devices in a mesh: wide: 8 (over y, x, core), narrow: 4 (over z).
Axes of the slice: x: 2, y: 2, z: 4, core: 2. Of those that a mesh axis runs over, the one named last changes fastest.
Arguments:
- pair_tokens: bfloat16 [32, 2, 128, 768], P(('wide', 'narrow')), may hold values from -6 to 6
- expert_ids: int32 [32, 256, 2], P(('wide', 'narrow')), may hold values from 0 to 7, all different within a row; in each aligned block of 256 rows (0 to 255, 256 to 511, ..., all dimensions but the last counted through in order) at most 68 rows name the same one
- positive: int32 [32], replicated, may hold values from 0 to 31, each once
- w_qkv: bfloat16 [768, 2304], replicated, may hold values from -0.21875 to 0.21875
- w_out: bfloat16 [768, 768], replicated, may hold values from -0.21875 to 0.21875
- w_router: bfloat16 [768, 8], replicated, may hold values from -0.21875 to 0.21875
- w_up: bfloat16 [8, 768, 3072], P('wide', None, 'narrow'), may hold values from -0.21875 to 0.21875
- w_down: bfloat16 [8, 3072, 768], P('wide', 'narrow'), may hold values from -0.109375 to 0.109375
Outputs:
- grad_up: float32 [8, 768, 3072], P('wide', None, 'narrow')
- grad_down: float32 [8, 3072, 768], P('wide', 'narrow')
Inputs may be any that keep to these rules, and one draw needn't show every extreme that they name: `expert_ids`: the two experts of a token differ. Among the 256 tokens of one device no expert is named more than 68 times, and in every draw some device names some expert exactly 68 times. Each document is the positive of exactly one query.
All inputs are finite; a program needn't handle non-finite values.
Results may differ from a plain program's by a relative error of at most 0.023.
Values may be sent and summed in bfloat16 or wider, within the bound.
No kernel may reach another device: no remote copies, remote signals or barrier semaphores. Data moves between devices by JAX's collectives and lax.ppermute only.
A program may use at most 128 MiB of HBM per device.

v0:
```python
import math

import jax
import jax.numpy as jnp
from jax import lax
from jax.sharding import PartitionSpec as P

HEADS = 12
HEAD_DIM = 64
SEQ = 128


epsilon = 1e-06
inverse_softmax_warmth = 20.0
loss_scale = 64.0


def rms_scaled(values):
    return values * lax.rsqrt(jnp.mean(values * values, axis=-1, keepdims=True) + epsilon)


def attention_block(tokens, w_qkv, w_out):
    count = tokens.shape[0]
    width = tokens.shape[1]
    normed = rms_scaled(tokens.astype(jnp.float32)).astype(jnp.bfloat16)
    project = jnp.dot(normed, w_qkv, preferred_element_type=jnp.float32)
    project = project.reshape(count // SEQ, SEQ, 3, HEADS, HEAD_DIM)
    query = rms_scaled(project[:, :, 0]).astype(jnp.bfloat16)
    keys_normed = rms_scaled(project[:, :, 1]).astype(jnp.bfloat16)
    values_cast = project[:, :, 2].astype(jnp.bfloat16)
    cosine_logit_matrix = jnp.einsum(
        "sqhe,skhe->shqk", query, keys_normed, preferred_element_type=jnp.float32
    ) / math.sqrt(HEAD_DIM)
    weights = jnp.exp(cosine_logit_matrix)
    weights = (weights / jnp.sum(weights, axis=-1, keepdims=True)).astype(jnp.bfloat16)
    mixed = jnp.einsum("shqk,skhe->sqhe", weights, values_cast, preferred_element_type=jnp.float32)
    mixed = mixed.astype(jnp.bfloat16).reshape(count, width)
    update = jnp.dot(mixed, w_out, preferred_element_type=jnp.float32)
    return (tokens.astype(jnp.float32) + update).astype(jnp.bfloat16)


def gate_pair(logits, picks):
    experts = logits.shape[-1]
    onehot = (picks[:, :, None] == jnp.arange(experts, dtype=jnp.int32)[None, None, :]).astype(
        jnp.float32
    )
    chosen_logits = jnp.sum(onehot * logits[:, None, :], axis=-1)
    first = jax.nn.sigmoid(chosen_logits[:, 0] - chosen_logits[:, 1])
    return jnp.stack([first, 1.0 - first], axis=1)


def slot_positions(picks, experts, capacity):
    flat = picks.reshape(-1)
    onehot = (flat[:, None] == jnp.arange(experts, dtype=jnp.int32)[None, :]).astype(jnp.int32)
    earlier = jnp.cumsum(onehot, axis=0) - onehot
    return flat * capacity + jnp.sum(earlier * onehot, axis=1)


def contract_rows(left, right):
    return lax.dot_general(
        left, right, (((0,), (0,)), ((), ())), preferred_element_type=jnp.float32
    )


def body(pair_tokens, expert_ids, positive, w_qkv, w_out, w_router, w_up, w_down):
    experts = lax.axis_size("wide")
    groups = lax.axis_size("narrow")
    pair_count = pair_tokens.shape[0]
    width = pair_tokens.shape[-1]
    tokens = pair_tokens.reshape(-1, width)
    count = tokens.shape[0]
    capacity = 17 * count // (8 * experts)
    picks = expert_ids.reshape(-1, 2)
    hidden_state = attention_block(tokens, w_qkv, w_out)
    normed = rms_scaled(hidden_state.astype(jnp.float32)).astype(jnp.bfloat16)
    logits = jnp.dot(normed, w_router, preferred_element_type=jnp.float32)
    gates = gate_pair(logits, picks)
    destination = slot_positions(picks, experts, capacity)
    outgoing = jnp.zeros((experts * capacity, width), jnp.bfloat16)
    outgoing = (
        outgoing.at[destination]
        .set(jnp.repeat(normed, 2, axis=0))
        .reshape(experts, capacity, width)
    )
    arrived = lax.all_to_all(outgoing, "wide", split_axis=0, concat_axis=0, tiled=True)
    up_local = w_up[0]
    down_local = w_down[0]
    slot_rows = lax.all_gather(arrived, "narrow", axis=0, tiled=True).reshape(-1, width)
    pre_act = jnp.dot(slot_rows, up_local, preferred_element_type=jnp.float32)
    activated = jax.nn.gelu(pre_act).astype(jnp.bfloat16)
    partial_value = jnp.dot(activated, down_local, preferred_element_type=jnp.float32)
    partial_value = partial_value.reshape(groups, experts * capacity, width)
    summed = lax.psum_scatter(
        partial_value.astype(jnp.bfloat16), "narrow", scatter_dimension=0, tiled=True
    )
    expert_out = summed.reshape(experts, capacity, width)
    returned = lax.all_to_all(expert_out, "wide", split_axis=0, concat_axis=0, tiled=True).reshape(
        experts * capacity, width
    )
    picked = returned[destination].reshape(count, 2, width)
    mixed = hidden_state.astype(jnp.float32) + jnp.sum(
        gates[:, :, None] * picked.astype(jnp.float32), axis=1
    )
    pooled = jnp.mean(mixed.reshape(pair_count, 2, SEQ, width), axis=2)
    length = jnp.sqrt(jnp.sum(pooled * pooled, axis=-1, keepdims=True) + epsilon)
    unit = pooled / length
    search_unit_vector = unit[:, 0]
    passage_unit_vector = unit[:, 1]
    start = lax.axis_index(("wide", "narrow")) * pair_count
    largest_score = lax.Precision.HIGHEST
    gathered_documents = lax.all_gather(passage_unit_vector, ("wide", "narrow"), axis=0, tiled=True)
    cosine_logit_matrix = (
        jnp.dot(search_unit_vector, gathered_documents.T, precision=largest_score)
        * inverse_softmax_warmth
    )
    probs = jnp.exp(cosine_logit_matrix)
    probs = probs / jnp.sum(probs, axis=1, keepdims=True)
    own_positive = lax.dynamic_slice_in_dim(positive, start, pair_count)
    target = (
        own_positive[:, None] == jnp.arange(gathered_documents.shape[0], dtype=jnp.int32)[None, :]
    ).astype(jnp.float32)
    logit_excess_matrix = (probs - target) * loss_scale
    search_embedding_adjoint = (
        jnp.dot(logit_excess_matrix, gathered_documents, precision=largest_score)
        * inverse_softmax_warmth
    )
    document_partials = (
        jnp.dot(logit_excess_matrix.T, search_unit_vector, precision=largest_score)
        * inverse_softmax_warmth
    )
    passage_embedding_adjoint = lax.psum_scatter(
        document_partials, ("wide", "narrow"), scatter_dimension=0, tiled=True
    )
    unit_grad = jnp.stack([search_embedding_adjoint, passage_embedding_adjoint], axis=1)
    pooled_grad = (unit_grad - unit * jnp.sum(unit * unit_grad, axis=-1, keepdims=True)) / length
    token_grad = jnp.broadcast_to(
        (pooled_grad / SEQ)[:, :, None, :], (pair_count, 2, SEQ, width)
    ).reshape(count, width)
    cotangent = (
        (gates[:, :, None] * token_grad[:, None, :]).astype(jnp.bfloat16).reshape(2 * count, width)
    )
    outgoing_grad = jnp.zeros((experts * capacity, width), jnp.bfloat16)
    outgoing_grad = outgoing_grad.at[destination].set(cotangent).reshape(experts, capacity, width)
    arrived_grad = lax.all_to_all(outgoing_grad, "wide", split_axis=0, concat_axis=0, tiled=True)
    grad_rows = lax.all_gather(arrived_grad, "narrow", axis=0, tiled=True).reshape(-1, width)
    down_grad = contract_rows(activated, grad_rows)
    act_grad = jnp.dot(grad_rows, down_local.T, preferred_element_type=jnp.float32)
    unused, pullback = jax.vjp(jax.nn.gelu, pre_act)
    pre_grad = pullback(act_grad)[0].astype(jnp.bfloat16)
    up_grad = contract_rows(slot_rows, pre_grad)
    return (up_grad[None], down_grad[None])


def solution(mesh):
    return jax.shard_map(
        body,
        mesh=mesh,
        in_specs=(
            P(("wide", "narrow"), None, None, None),
            P(("wide", "narrow"), None, None),
            P(),
            P(),
            P(),
            P(),
            P("wide", None, "narrow"),
            P("wide", "narrow", None),
        ),
        out_specs=(P("wide", None, "narrow"), P("wide", "narrow", None)),
        check_vma=False,
    )
```

profile of v0, /device:TPU:0, one launch (start us, length us, event | category | flops | bytes accessed | tf_op | source)
XLA Modules:
  0.0 562.9 jit_solution(5658135596952322082)
XLA Ops:
  13.7 5.8 %copy.39 = bf16[768,2304]{0,1:T(8,128)(2,1)} copy(bf16[768,2304]{1,0:T(8,128)(2,1)} %param.11) | data formatting | bytes 7077888 | tf_op args[3]
  19.4 3.3 fusion.33
  23.0 1.6 multiply_exponential_fusion
  24.6 3.0 fusion.14
  27.6 1.4 copy.41
  29.1 1.9 multiply_reduce_fusion.1
  33.7 3.4 scatter_custom_fusion
  37.3 18.6 %all_to_all.15 = bf16[8,68,768]{2,1,0:T(8,128)(2,1)S(1)} all-to-all(bf16[8,68,768]{2,1,0:T(8,128)(2,1)S(1)} %reshape.360), channel_id=1, replica_groups=mesh['wide'=8,'narrow'=4] {'wide'}, dimensions={0} | all-to-all | bytes 1671168 | tf_op jit(solution)/shard_map/all_to_all | solution.py:85
  57.2 66.0 %all-gather.4.cloned.1.call-done = bf16[32,68,768]{2,0,1:T(8,128)(2,1)} async-done(((bf16[8,68,768]{2,0,1:T(8,128)(2,1)}), bf16[32,68,768]{2,0,1:T(8,128)(2,1)}) %all-gather.4.cloned.1.call-update) | async-done | bytes 3342352 | tf_op jit(solution)/shard_map/all_gather | solution.py:88
  123.2 5.6 copy.43
  128.8 5.5 reshape.361
  134.2 8.6 %multiply_convert_fusion = (bf16[2176,768]{1,0:T(8,128)(2,1)S(1)}, f32[2176,768]{1,0:T(8,128)}) fusion(bf16[2176,768]{1,0:T(8,128)(2,1)} %reshape.361, bf16[1,768,768]{2,1,0:T(8,128)(2,1)S(1)} %copy-done), kind=kOutput, calls=%fused_computation.12 | convolution fusion | flops 2581954560 | bytes 14548992 | tf_op jit(solution)/shard_map/dot_general | solution.py:89
  142.9 1.7 copy-done.12
  144.5 4.2 convolution_convert_fusion
  148.7 62.1 %reduce-scatter.2.cloned.1.call-done = bf16[1,544,768]{2,1,0:T(8,128)(2,1)} async-done(((bf16[4,544,768]{2,1,0:T(8,128)(2,1)}), bf16[1,544,768]{2,1,0:T(8,128)(2,1)}) %reduce-scatter.2.cloned.1.call-update) | async-done | bytes 835600 | tf_op jit(solution)/shard_map/reduce_scatter | solution.py:93
  210.9 2.1 reshape.362
  213.0 3.7 all-to-all-start.1
  218.2 12.1 %all-to-all-done.1 = bf16[8,68,768]{2,1,0:T(8,128)(2,1)S(1)} async-done(((bf16[8,68,768]{2,1,0:T(8,128)(2,1)}), bf16[8,68,768]{2,1,0:T(8,128)(2,1)S(1)}, u32[]{:S(2)}, u32[]{:S(2)}) %all-to-all-start.1) | async-done | bytes 835616 | tf_op jit(solution)/shard_map/all_to_all | solution.py:97
  230.4 2.7 gather_fusion
  233.1 2.2 reshape.369
  235.4 1.9 multiply_reduce_fusion
  237.6 66.0 %all-gather = f32[32,1,768]{2,1,0:T(1,128)S(1)} all-gather(f32[1,1,768]{2,1,0:T(1,128)S(1)} %get-tuple-element.6), channel_id=2, replica_groups=mesh['wide'=8,'narrow'=4] {'wide','narrow'}, dimensions={0}, use_global_device_ids=true | all-gather | bytes 101376 | tf_op jit(solution)/shard_map/all_gather | solution.py:111
  306.8 118.0 %all-reduce.3.cloned.1.call-done = f32[32,768]{1,0:T(8,128)} async-done(((f32[32,768]{1,0:T(8,128)}), f32[32,768]{1,0:T(8,128)}) %all-reduce.3.cloned.1.call-update) | async-done | bytes 98320
  426.6 1.7 mul.253
  428.3 2.4 mul.254
  430.6 3.6 scatter_custom_fusion.1
  435.6 16.5 %all_to_all.16 = bf16[8,68,768]{2,1,0:T(8,128)(2,1)S(1)} all-to-all(bf16[8,68,768]{2,1,0:T(8,128)(2,1)S(1)} %reshape.366), channel_id=1, replica_groups=mesh['wide'=8,'narrow'=4] {'wide'}, dimensions={0} | all-to-all | bytes 1671168 | tf_op jit(solution)/shard_map/all_to_all | solution.py:144
  453.1 66.4 %all-gather.6.cloned.1.call-done = bf16[32,68,768]{2,0,1:T(8,128)(2,1)} async-done(((bf16[8,68,768]{2,0,1:T(8,128)(2,1)}), bf16[32,68,768]{2,0,1:T(8,128)(2,1)}) %all-gather.6.cloned.1.call-update) | async-done | bytes 3342352 | tf_op jit(solution)/shard_map/all_gather | solution.py:145
  519.6 5.6 copy.47
  525.2 5.7 %reshape.367 = bf16[2176,768]{1,0:T(8,128)(2,1)} reshape(bf16[32,68,768]{2,1,0:T(8,128)(2,1)} %copy.47) | data formatting | bytes 6684672 | tf_op jit(solution)/shard_map/reshape | solution.py:145
  530.9 7.4 %convolution_bitcast_fusion = f32[1,768,768]{2,1,0:T(8,128)} fusion(bf16[2176,768]{1,0:T(8,128)(2,1)} %copy-done.12, bf16[2176,768]{1,0:T(8,128)(2,1)} %reshape.367), kind=kOutput, calls=%fused_computation.15 | convolution fusion | flops 2566914048 | bytes 9043968 | tf_op jit(solution)/shard_map/dot_general | solution.py:60
  538.4 17.5 %fusion.9 = f32[1,768,768]{2,1,0:T(8,128)} fusion(bf16[2176,768]{1,0:T(8,128)(2,1)} %reshape.361, f32[2176,768]{1,0:T(8,128)} %get-tuple-element.11, bf16[2176,768]{1,0:T(8,128)(2,1)} %reshape.367, bf16[1,768,768]{2,1,0:T(8,128)(2,1)S(1)} %copy-done.10), kind=kOutput, calls=%fused_computation.16 | convolution fusion | flops 5167251456 | bytes 16908288 | tf_op jit(solution)/shard_map/dot_general | solution.py:60
  (85 shorter events, 20.1 us)
Async XLA Ops:
  7.2 127.1 %copy-start = (bf16[1,768,768]{2,1,0:T(8,128)(2,1)S(1)}, bf16[1,768,768]{2,1,0:T(8,128)(2,1)}, u32[]{:S(2)}) copy-start(bf16[1,768,768]{2,1,0:T(8,128)(2,1)} %param.14) | copy-start | bytes 3538948
  7.2 116.0 %all-gather.4.cloned.1.call-start = ((), (), s32[]{:S(2)}) async-start(), calls=%async_computation.4 | async-start | bytes 4177920 | tf_op jit(solution)/shard_map/all_gather | solution.py:88
  13.7 5.8 %copy-start.6 = (s32[8,5]{0,1:T(8,128)}, s32[8,5]{0,1:T(8,128)S(1)}, u32[]{:S(2)}) copy-start(s32[8,5]{0,1:T(8,128)S(1)} %reduce-window.9) | copy-start | bytes 484
  29.0 4.6 slice-start
  29.1 4.6 copy-start.8
  29.1 4.6 copy-start.7
  31.0 0.9 copy-start.2
  57.0 153.9 %reduce-scatter.2.cloned.1.call-start = ((), (), s32[]{:S(2)}) async-start(), calls=%async_computation.5 | async-start | bytes 4177920 | tf_op jit(solution)/shard_map/reduce_scatter | solution.py:93
  134.2 10.3 %copy-start.9 = (bf16[1,768,768]{2,1,0:T(8,128)(2,1)S(1)}, bf16[1,768,768]{2,1,0:T(8,128)(2,1)}, u32[]{:S(2)}) copy-start(bf16[1,768,768]{2,1,0:T(8,128)(2,1)} %param.15) | copy-start | bytes 3538948
  142.9 1.7 copy-start.12
  148.7 68.2 %copy-start.5 = (bf16[768,8]{0,1:T(8,128)(2,1)S(1)}, bf16[768,8]{0,1:T(8,128)(2,1)}, u32[]{:S(2)}) copy-start(bf16[768,8]{0,1:T(8,128)(2,1)} %param.13) | copy-start | bytes 36868
  148.7 68.4 %copy-start.4 = (s32[1,256,2]{1,2,0:T(2,128)S(1)}, s32[1,256,2]{1,2,0:T(2,128)}, u32[]{:S(2)}) copy-start(s32[1,256,2]{1,2,0:T(2,128)} %param.9) | copy-start | bytes 6148
  148.7 68.8 %copy-start.11 = (s32[32]{0:T(128)S(1)}, s32[32]{0:T(128)}, u32[]{:S(2)}) copy-start(s32[32]{0:T(128)} %param.10) | copy-start | bytes 388
  213.0 17.3 %all-to-all-start.1 = ((bf16[8,68,768]{2,1,0:T(8,128)(2,1)}), bf16[8,68,768]{2,1,0:T(8,128)(2,1)S(1)}, u32[]{:S(2)}, u32[]{:S(2)}) async-start(bf16[8,68,768]{2,1,0:T(8,128)(2,1)} %reshape.362), calls=%async_computation.2 | async-start | bytes 1769472 | tf_op jit(solution)/shard_map/all_to_all | solution.py:97
  216.6 208.1 %all-reduce.3.cloned.1.call-start = ((), (), s32[]{:S(2)}) async-start(), calls=%async_computation.7 | async-start | bytes 196608
  233.1 4.2 copy-start.3
  306.7 212.9 %all-gather.6.cloned.1.call-start = ((), (), s32[]{:S(2)}) async-start(), calls=%async_computation.6 | async-start | bytes 4177920 | tf_op jit(solution)/shard_map/all_gather | solution.py:145
  530.9 7.4 %copy-start.10 = (bf16[1,768,768]{2,1,0:T(8,128)(2,1)S(1)}, bf16[1,768,768]{2,1,0:T(8,128)(2,1)}, u32[]{:S(2)}) copy-start(bf16[1,768,768]{2,1,0:T(8,128)(2,1)} %param.15) | copy-start | bytes 3538948
  538.4 17.5 %copy-start.1 = (bf16[1,768,768]{2,1,0:T(8,128)(2,1)S(1)}, bf16[1,768,768]{2,1,0:T(8,128)(2,1)}, u32[]{:S(2)}) copy-start(bf16[1,768,768]{2,1,0:T(8,128)(2,1)} %param.14) | copy-start | bytes 3538948
Sparse Core Ops, SparseCore 0:
  57.1 66.0 all-gather.3
  148.8 61.9 reduce-scatter.1
  306.8 117.9 all-reduce.2
  453.3 66.2 all-gather.5
where the time goes:
time: 570 us; the launch traced here: 563 us
  waiting for transfers between devices  325 us (57%)
  blocking collectives  101 us (18%)
  local copies, waits for them, and re-layouts  57.1 us (10%)
  matrix products  48.8 us (9%)
  between operations  14.5 us (3%)
  other arithmetic  12.4 us (2%)
    unnamed x5, waiting for transfers between devices  118 us
    all_gather x1, waiting for transfers between devices, body(): lax.all_gather(arrived_grad, 'narrow', axis=0, tiled=True)  66.4 us
    all_gather x1, waiting for transfers between devices, body(): lax.all_gather(arrived, 'narrow', axis=0, tiled=True).reshape(-1, width)  66 us
    all_gather x1, blocking collectives, body(): lax.all_gather(passage_unit_vector, ('wide', 'narrow'), axis=0, tiled=True)  66 us
    reduce_scatter x1, waiting for transfers between devices, body(): lax.psum_scatter(partial_value.astype(jnp.bfloat16), 'narrow', scatter_di...  62.1 us
    dot_general x2, matrix products, contract_rows(): lax.dot_general(left, right, (((0,), (0,)), ((), ())), preferred_element_...  25 us
    all_to_all x1, blocking collectives, body(): lax.all_to_all(outgoing, 'wide', split_axis=0, concat_axis=0, tiled=True)  18.6 us
    all_to_all x1, blocking collectives, body(): lax.all_to_all(outgoing_grad, 'wide', split_axis=0, concat_axis=0, tiled=...  16.5 us
  transfers between devices with their start and end apart: 5, of which 5 were waited for; matrix products, arithmetic and copies ran while one was open for 0% of the time, Pallas kernels for 0%

commit v1 on v0

v1 whole, which is shorter than its diff:
```python
import functools

import jax
import jax.numpy as jnp
from jax import lax
from jax.experimental import pallas as pl
from jax.experimental.pallas import tpu as pltpu
from jax.sharding import PartitionSpec as P

HEADS = 12
HEAD_DIM = 64
SEQ = 128
EPS = 1e-06
WARMTH = 20.0
LOSS_SCALE = 64.0
LANES = 128
INFO = 8
SELECT_WEIGHT = 1000
GELU_C = 0.7978845608028654
GELU_D = 0.044715 * GELU_C
BF16 = jnp.bfloat16
F32 = jnp.float32


def dot(left, right, contract=(1, 0)):
    return lax.dot_general(
        left, right, (((contract[0],), (contract[1],)), ((), ())), preferred_element_type=F32
    )


def split_dot(left, right, contract):
    left_high, right_high = left.astype(BF16), right.astype(BF16)
    left_low = (left - left_high.astype(F32)).astype(BF16)
    right_low = (right - right_high.astype(F32)).astype(BF16)
    return (
        dot(left_low, right_high, contract) + dot(left_high, right_low, contract)
    ) + dot(left_high, right_high, contract)


def iota(shape, axis):
    return lax.broadcasted_iota(jnp.int32, shape, axis)


def rms_scaled(values):
    return values * lax.rsqrt(jnp.mean(values * values, axis=-1, keepdims=True) + EPS)


def dispatch(rows, info, experts, block, capacity):
    count = rows.shape[0]
    first, second, slot_a, slot_b, gate_a, gate_b = (info[i : i + 1] for i in range(6))
    place = iota((experts * block, count), 0).astype(F32)
    chosen = (place == first * block + slot_a) | (place == second * block + slot_b)
    out = dot(jnp.where(chosen, 1.0, 0.0).astype(BF16), rows)
    expert = iota((experts, count), 0).astype(F32)
    owned = jnp.concatenate(
        [jnp.where(expert == first, gate_a, 0.0), jnp.where(expert == second, gate_b, 0.0)], axis=1
    ).astype(BF16)
    lane = iota((LANES, count), 0).astype(F32)
    slots = jnp.concatenate(
        [jnp.where(lane == slot_a, 1.0, 0.0), jnp.where(lane == slot_b, 1.0, 0.0)], axis=1
    ).astype(BF16)
    gates = dot(owned, slots, (1, 1))
    gate_row = iota((block, LANES), 0) == capacity
    blocks = []
    for e in range(experts):
        part = out[e * block : (e + 1) * block]
        head = jnp.where(gate_row, gates[e : e + 1], part[:, :LANES])
        blocks.append(jnp.concatenate([head, part[:, LANES:]], axis=1))
    return blocks


def front_kernel(
    tokens_hbm, ids_hbm, router_hbm, qkv_hbm, out_hbm,
    half_ref, whole_ref, sums_ref,
    tokens_ref, ids_ref, router_ref, qkv_ref, w_out_ref, mixed_ref, sems,
):
    count, width = tokens_ref.shape
    parts = [
        pltpu.make_async_copy(
            qkv_hbm.at[:, pl.ds(i * width, width)], qkv_ref.at[i], sems.at[i]
        )
        for i in range(3)
    ]
    last = pltpu.make_async_copy(out_hbm, w_out_ref, sems.at[3])
    first = pltpu.make_async_copy(tokens_hbm, tokens_ref, sems.at[4])
    small = [
        pltpu.make_async_copy(ids_hbm, ids_ref, sems.at[5]),
        pltpu.make_async_copy(router_hbm, router_ref, sems.at[6]),
    ]
    for load in [first, *parts, last, *small]:
        load.start()
    first.wait()
    tokens = tokens_ref[...].astype(F32)
    normed = rms_scaled(tokens).astype(BF16)
    half = iota((SEQ, LANES), 1) < HEAD_DIM
    wide = 2 * LANES
    same_head = jnp.where(
        iota((wide, wide), 0) // HEAD_DIM == iota((wide, wide), 1) // HEAD_DIM, 1.0, 0.0
    ).astype(BF16)

    def head_scaled(part, scale):
        out = []
        for start in range(0, width, wide):
            some = part[:, start : start + wide]
            squares = some * some
            high = squares.astype(BF16)
            low = (squares - high.astype(F32)).astype(BF16)
            level = dot(high, same_head) + dot(low, same_head)
            out.append(some * (lax.rsqrt(level * (1.0 / HEAD_DIM) + EPS) * scale))
        return jnp.concatenate(out, axis=1)

    parts[0].wait()
    query = head_scaled(dot(normed, qkv_ref[0]), HEAD_DIM ** -0.5)
    parts[1].wait()
    keys = head_scaled(dot(normed, qkv_ref[1]), 1.0).astype(BF16)
    parts[2].wait()
    values = dot(normed, qkv_ref[2]).astype(BF16)
    ones = jnp.ones((SEQ, LANES), BF16)
    pieces = [
        (slice(seq * SEQ, (seq + 1) * SEQ), slice(start, start + LANES))
        for start in range(0, width, LANES)
        for seq in range(count // SEQ)
    ]
    scores = []
    for at in pieces:
        one = query[at]
        both = jnp.concatenate([jnp.where(half, one, 0.0), jnp.where(half, 0.0, one)], axis=0)
        scores.append(dot(both.astype(BF16), keys[at], (1, 1)))
    weights = [jnp.exp(score).astype(BF16) for score in scores]
    summed = [
        dot(weight, jnp.concatenate([values[at], ones], axis=1))
        for at, weight in zip(pieces, weights)
    ]
    for at, both in zip(pieces, summed):
        shares = both[:, :LANES] / both[:, LANES:]
        mixed_ref[at] = jnp.where(half, shares[:SEQ], shares[SEQ:]).astype(BF16)
    last.wait()
    hidden = (tokens + dot(mixed_ref[...], w_out_ref[...])).astype(BF16).astype(F32)
    for seq in range(count // SEQ):
        sums_ref[seq : seq + 1] = jnp.sum(
            hidden[seq * SEQ : (seq + 1) * SEQ], axis=0, keepdims=True
        )
    normed = rms_scaled(hidden).astype(BF16)
    for load in small:
        load.wait()
    logits = dot(router_ref[...], normed, (1, 1))
    ids = ids_ref[...]
    expert = iota(logits.shape, 0)
    named_a = jnp.where(ids[0:1] == expert, 1.0, 0.0)
    named_b = jnp.where(ids[1:2] == expert, 1.0, 0.0)
    logit_a = jnp.sum(named_a * logits, axis=0, keepdims=True)
    logit_b = jnp.sum(named_b * logits, axis=0, keepdims=True)
    gate_a = jax.nn.sigmoid(logit_a - logit_b)
    sign = jnp.where(iota((1, count), 1) < SEQ, 1.0, -1.0)
    earlier = jnp.where(iota((count, count), 0) < iota((count, count), 1), 1.0, 0.0).astype(BF16)
    before = dot((named_a + named_b).astype(BF16), earlier)
    info = jnp.concatenate(
        [
            ids.astype(F32),
            jnp.sum(named_a * before, axis=0, keepdims=True),
            jnp.sum(named_b * before, axis=0, keepdims=True),
            gate_a * sign,
            (1.0 - gate_a) * sign,
            jnp.zeros((INFO - 6, count), F32),
        ],
        axis=0,
    )
    for ref in (half_ref, whole_ref):
        near = ref.shape[1]
        tail = jnp.concatenate([info, jnp.zeros((INFO, near - count), F32)], axis=1)
        ref[...] = jnp.concatenate([normed[:, :near], tail.astype(BF16)], axis=0)


def own_kernel(experts, block, capacity, payload_ref, near_ref, far_ref):
    payload = payload_ref[...]
    count, half = payload.shape[0] - INFO, near_ref.shape[-1]
    info = payload[count:, :count].astype(F32)
    blocks = dispatch(payload[:count], info, experts, block, capacity)
    for e in range(experts):
        near_ref[e] = blocks[e][:, :half].astype(BF16)
        far_ref[e] = blocks[e][:, half:].astype(BF16)


def select_kernel(experts, block, capacity, *refs):
    steps = (len(refs) - 2) // 2
    shards, out_hbm, parts, sems = refs[:steps], refs[steps], refs[steps + 1 : -1], refs[-1]
    start, stores = 0, []
    for i, (shard_ref, part_ref) in enumerate(zip(shards, parts)):
        shard = shard_ref[...]
        count, near = shard.shape[0] - INFO, shard.shape[1]
        info = shard[count:, :count].astype(F32)
        blocks = dispatch(shard[:count], info, experts, block, capacity)
        for e in range(experts):
            part_ref[e] = blocks[e].astype(BF16)
        stores.append(
            pltpu.make_async_copy(part_ref, out_hbm.at[:, :, pl.ds(start, near)], sems.at[i])
        )
        stores[-1].start()
        start += near
    for store in stores:
        store.wait()


def gelu_parts(pre):
    square = pre * pre
    return square, jnp.tanh(pre * (GELU_C + GELU_D * square))


def gelu_slope(pre, square, turn):
    inner = pre * (GELU_C + 3.0 * GELU_D * square)
    return 0.5 * (1.0 + turn) + 0.5 * inner * (1.0 - turn * turn)


def gate_matrix(head, origin, experts, groups, block, capacity):
    devices = experts * groups
    column = iota((block, 2 * devices), 1)
    tile, row = capacity // 8 * 8, capacity % 8
    found = [
        head[w * block + tile : w * block + tile + 8][row : row + 1] for w in range(experts)
    ]
    found.append(jnp.zeros((LANES - experts, LANES), F32))
    turned = jnp.concatenate(found, axis=0).T[:block]
    pieces = []
    for w in range(experts):
        gate = turned[:, w : w + 1]
        device = w * groups + origin
        pieces.append(
            jnp.where(
                column == device,
                jnp.maximum(gate, 0.0),
                jnp.where(column == device + devices, jnp.maximum(-gate, 0.0), 0.0),
            )
        )
    return jnp.concatenate(pieces, axis=0).astype(BF16)


def shard_rows(near_ref):
    return jnp.concatenate(
        [near_ref[w].astype(F32) for w in range(near_ref.shape[0])], axis=0
    )


def own_expert_kernel(
    experts, groups, block, capacity,
    near_ref, far_ref, up_ref, slope_ref, gates_ref, sums_ref,
):
    pre = dot(jnp.concatenate([near_ref[...], far_ref[...]], axis=1), up_ref[...])
    square, turn = gelu_parts(pre)
    act = (0.5 * pre * (1.0 + turn)).astype(BF16)
    slope_ref[...] = gelu_slope(pre, square, turn).astype(BF16)
    head = near_ref[:, :LANES].astype(F32)
    gates = gate_matrix(head, lax.axis_index("narrow"), experts, groups, block, capacity)
    gates_ref[...] = gates
    sums_ref[...] = dot(gates, act, (0, 0))


def expert_kernel(experts, groups, block, capacity, nears, *refs):
    near_hbm = refs[0]
    count = groups - 1
    owners = [i for i in range(count) if nears[i] < max(nears)]
    far_hbms = refs[1 : 1 + len(owners)]
    (
        up_hbm, down_hbm, own_sums_hbm, pre_hbm, gates_hbm, sums_hbm, partial_hbm,
        partial_ref, up_ref, down_ref, pre_ref, gates_ref, sums_ref, *parts, sems,
    ) = refs[1 + len(owners) :]
    near_refs, far_refs = parts[:count], parts[count:]
    here = lax.axis_index("narrow")
    size = experts * block
    devices = experts * groups
    slots = iter(range(sems.shape[0]))

    def copy(source, target):
        return pltpu.make_async_copy(source, target, sems.at[next(slots)])

    weights = [copy(up_hbm, up_ref), copy(down_hbm, down_ref)]
    own_sums = copy(own_sums_hbm, sums_ref)
    loads = []
    for i in range(count):
        columns = pl.ds(sum(nears[:i]), nears[i])
        loads.append([copy(near_hbm.at[:, :, columns], near_refs[i])])
        if i in owners:
            loads[i].append(copy(far_hbms[owners.index(i)], far_refs[owners.index(i)]))
    ats = [pl.ds(i * size, size) for i in range(count)]
    stores = [copy(pre_ref.at[at], pre_hbm.at[at]) for at in ats]
    gate_stores = [copy(gates_ref.at[at], gates_hbm.at[at]) for at in ats]
    sums_store = copy(sums_ref, sums_hbm)
    partial_store = copy(partial_ref, partial_hbm)
    for load in [weights[0], *sum(loads, []), own_sums, weights[1]]:
        load.start()
    weights[0].wait()
    cuts = [slice(start, start + size // 2) for start in (0, size // 2)]
    for i in range(count):
        at = slice(i * size, (i + 1) * size)
        for load in loads[i]:
            load.wait()
        gathered = shard_rows(near_refs[i])
        rows = gathered.astype(BF16)
        if i in owners:
            rows = jnp.concatenate([rows, far_refs[owners.index(i)][...]], axis=1)
        acts = []
        for cut in cuts:
            pre = dot(rows[cut], up_ref[...])
            pre_ref[i * size + cut.start : i * size + cut.stop] = pre.astype(BF16)
            turn = gelu_parts(pre)[1]
            acts.append((0.5 * pre * (1.0 + turn)).astype(BF16))
        stores[i].start()
        act = jnp.concatenate(acts, axis=0)
        origin = lax.rem(here + count - i, groups)
        gates = gate_matrix(gathered[:, :LANES], origin, experts, groups, block, capacity)
        gates_ref[at] = gates
        gate_stores[i].start()
        part = dot(gates, act, (0, 0))
        if i == 0:
            own_sums.wait()
            total = sums_ref[...]
        total = total + part
    sums_ref[...] = total
    sums_store.start()
    high = total.astype(BF16)
    low = (total - high.astype(F32)).astype(BF16)
    weights[1].wait()
    pooled = dot(jnp.concatenate([high, low], axis=0), down_ref[...])
    pooled = pooled[: 2 * devices] + pooled[2 * devices :]
    for device in range(devices):
        pair = [pooled[i : i + 1] for i in (device, device + devices)]
        partial_ref[device] = jnp.concatenate(pair, axis=0).astype(BF16)
    partial_store.start()
    for store in [*stores, *gate_stores, sums_store, partial_store]:
        store.wait()


def slope_kernel(pre_hbm, slope_hbm, pre_ref, slope_ref, sems):
    parts = sems.shape[1]
    size = pre_ref.shape[0] // parts
    cuts = [pl.ds(i * size, size) for i in range(parts)]
    loads = [
        pltpu.make_async_copy(pre_hbm.at[cut], pre_ref.at[cut], sems.at[0, i])
        for i, cut in enumerate(cuts)
    ]
    stores = [
        pltpu.make_async_copy(slope_ref.at[cut], slope_hbm.at[cut], sems.at[1, i])
        for i, cut in enumerate(cuts)
    ]
    for load in loads:
        load.start()
    for cut, load, store in zip(cuts, loads, stores):
        load.wait()
        pre = pre_ref[cut].astype(F32)
        slope_ref[cut] = gelu_slope(pre, *gelu_parts(pre)).astype(BF16)
        store.start()
    for store in stores:
        store.wait()


def turn_kernel(nears, *refs):
    count = len(nears)
    owners = [i for i in range(count) if nears[i] < max(nears)]
    hbms, (turned_hbm, *refs) = refs[: 3 + len(owners)], refs[3 + len(owners) :]
    refs, turned_ref, sems = refs[: len(hbms)], refs[-2], refs[-1]
    loads = [
        pltpu.make_async_copy(hbm, ref, sems.at[i]) for i, (hbm, ref) in enumerate(zip(hbms, refs))
    ]
    for load in loads:
        load.start()
    near_ref, far_refs = refs[2], refs[3:]
    size = refs[0].shape[0]
    stores = []
    loads[0].wait()
    loads[1].wait()
    rows = jnp.concatenate([refs[0][...], refs[1][...]], axis=1)
    turned_ref[:, :size] = rows.T
    loads[2].wait()
    for i, near in enumerate(nears, 1):
        start = sum(nears[: i - 1])
        rows = jnp.concatenate(
            [near_ref[w, :, start : start + near].astype(F32) for w in range(near_ref.shape[0])],
            axis=0,
        ).astype(BF16)
        if i - 1 in owners:
            loads[3 + owners.index(i - 1)].wait()
            rows = jnp.concatenate([rows, far_refs[owners.index(i - 1)][...]], axis=1)
        turned_ref[:, i * size : (i + 1) * size] = rows.T
        if i % 2:
            cut = pl.ds((i - 1) * size, 2 * size)
            stores.append(
                pltpu.make_async_copy(
                    turned_ref.at[:, cut], turned_hbm.at[:, cut], sems.at[len(hbms) + i // 2]
                )
            )
            stores[-1].start()
    for store in stores:
        store.wait()


def pool_kernel(parts_ref, own_ref, out_ref):
    total = (jnp.sum(parts_ref[...].astype(F32), axis=0) + own_ref[...]) * (1.0 / SEQ)
    out_ref[...] = jnp.broadcast_to(total.astype(BF16)[None], out_ref.shape)


def backward_kernel(
    pooled_hbm, positive_hbm, gates_own_hbm, gates_hbm, sums_hbm, down_w_hbm,
    turned_hbm, slope_own_hbm, slope_hbm, up_hbm, down_hbm,
    pooled_ref, positive_ref, gates_ref, sums_ref, down_ref, turned_ref, slope_ref, pre_grad_ref, up_grad_ref, down_grad_ref, sems,
):
    width = down_ref.shape[1]
    devices = pooled_ref.shape[0]
    size = slope_own_hbm.shape[0]
    total = slope_ref.shape[0]
    loads = [
        pltpu.make_async_copy(slope_own_hbm, slope_ref.at[pl.ds(0, size)], sems.at[0]),
        pltpu.make_async_copy(slope_hbm, slope_ref.at[pl.ds(size, total - size)], sems.at[1]),
        pltpu.make_async_copy(turned_hbm, turned_ref, sems.at[2]),
        pltpu.make_async_copy(down_w_hbm, down_ref, sems.at[3]),
        pltpu.make_async_copy(sums_hbm, sums_ref, sems.at[4]),
        pltpu.make_async_copy(gates_own_hbm, gates_ref.at[pl.ds(0, size)], sems.at[5]),
        pltpu.make_async_copy(gates_hbm, gates_ref.at[pl.ds(size, total - size)], sems.at[6]),
    ]
    count = sems.shape[0]
    first = [
        pltpu.make_async_copy(pooled_hbm, pooled_ref, sems.at[count - 2]),
        pltpu.make_async_copy(positive_hbm, positive_ref, sems.at[count - 1]),
    ]
    for load in [*first, *loads[3:], *loads[:3]]:
        load.start()
    for load in first:
        load.wait()

    def unit_of(pooled):
        length = jnp.sqrt(jnp.sum(pooled * pooled, axis=1, keepdims=True) + EPS)
        return pooled / length, length

    pooled = pooled_ref[...].astype(F32)
    query, query_length = unit_of(pooled[:, 0])
    document, document_length = unit_of(pooled[:, 1])
    powers = jnp.exp(split_dot(query, document, (1, 1)) * WARMTH)
    probs = powers / jnp.sum(powers, axis=1, keepdims=True)
    row, column = iota((devices, devices), 0), iota((devices, devices), 1)
    chosen = jnp.where(positive_ref[...] == row, 1.0, 0.0).astype(BF16)
    target = dot(jnp.where(row == column, 1.0, 0.0).astype(BF16), chosen, (1, 1))
    excess = (probs - target) * LOSS_SCALE
    query_grad = split_dot(excess, document, (1, 0)) * WARMTH
    document_grad = split_dot(excess, query, (0, 0)) * WARMTH

    def pooled_grad(unit, grad, length):
        return (grad - unit * jnp.sum(unit * grad, axis=1, keepdims=True)) / (length * SEQ)

    token_grad = jnp.concatenate(
        [
            pooled_grad(query, query_grad, query_length),
            pooled_grad(document, document_grad, document_length),
        ],
        axis=0,
    ).astype(BF16)
    loads[3].wait()
    loads[4].wait()
    hidden_grad = dot(token_grad, down_ref[...], (1, 1)).astype(BF16)
    down_grad_ref[...] = dot(sums_ref[...].astype(BF16), token_grad, (0, 0))
    stores = [pltpu.make_async_copy(down_grad_ref, down_hbm, sems.at[7])]
    stores[0].start()
    for i in (5, 6, 0, 1):
        loads[i].wait()
    for start in range(0, total, size // 2):
        at = slice(start, start + size // 2)
        act_grad = dot(gates_ref[at], hidden_grad)
        pre_grad_ref[at] = (act_grad * slope_ref[at].astype(F32)).astype(BF16)
    loads[2].wait()
    tile = column_tile(pre_grad_ref.shape[1])
    for i, start in enumerate(range(0, pre_grad_ref.shape[1], tile)):
        cols = slice(start, start + tile)
        up_grad_ref[:, cols] = dot(turned_ref[...], pre_grad_ref[:, cols])
        store = pltpu.make_async_copy(
            up_grad_ref.at[:, pl.ds(start, tile)],
            up_hbm.at[:, pl.ds(start, tile)],
            sems.at[8 + i],
        )
        store.start()
        stores.append(store)
    for store in stores:
        store.wait()


MIB = 1024 * 1024


def column_tile(size):
    return 2 * LANES if size % (2 * LANES) == 0 else LANES


def call(kernel, outs, args, spaces, out_spaces=None, scratch=(), flops=0, vmem=60):
    outs = tuple(jax.ShapeDtypeStruct(s, d) for s, d in outs)
    out_spaces = out_spaces or "v" * len(outs)
    space = {"v": pltpu.VMEM, "s": pltpu.SMEM, "a": pl.ANY}
    moved = sum(x.size * jnp.dtype(x.dtype).itemsize for x in tuple(args) + outs)
    return pl.pallas_call(
        kernel,
        out_shape=outs,
        in_specs=[pl.BlockSpec(memory_space=space[k]) for k in spaces],
        out_specs=tuple(pl.BlockSpec(memory_space=space[k]) for k in out_spaces),
        scratch_shapes=[pltpu.VMEM(*x) if isinstance(x, tuple) else x for x in scratch],
        compiler_params=pltpu.CompilerParams(vmem_limit_bytes=vmem * MIB),
        cost_estimate=pl.CostEstimate(flops=flops, bytes_accessed=moved, transcendentals=0),
    )(*args)


def body(pair_tokens, expert_ids, positive, w_qkv, w_out, w_router, w_up, w_down):
    experts = lax.axis_size("wide")
    groups = lax.axis_size("narrow")
    devices = experts * groups
    width = pair_tokens.shape[-1]
    tokens = pair_tokens.reshape(-1, width)
    count = tokens.shape[0]
    capacity = 17 * count // (8 * experts)
    block = -(-(capacity + 1) // 8) * 8
    half = width // 2
    nears = [width if 2 * step == groups else half for step in range(1, groups)]
    size = experts * block
    hidden = w_up.shape[2]
    up, down = w_up[0], w_down[0]

    def from_behind(array, step):
        return lax.ppermute(array, "narrow", [(i, (i + step) % groups) for i in range(groups)])

    payload_half, payload, own_sum = call(
        front_kernel,
        [((count + INFO, half), BF16), ((count + INFO, width), BF16), ((2, width), F32)],
        (tokens, expert_ids.reshape(-1, 2).T, w_router.T, w_qkv, w_out),
        "aaaaa",
        scratch=[
            ((count, width), BF16),
            ((2, count), jnp.int32),
            ((experts, width), BF16),
            ((3, width, width), BF16),
            ((width, width), BF16),
            ((count, width), BF16),
            pltpu.SemaphoreType.DMA((7,)),
        ],
        flops=2 * count * width * width * 5,
    )
    shards = [
        from_behind(payload if near == width else payload_half, step)
        for step, near in enumerate(nears, 1)
    ]
    own_halves = call(
        functools.partial(own_kernel, experts, block, capacity),
        [((experts, block, half), BF16), ((experts, block, width - half), BF16)],
        (payload,),
        "v",
        flops=2 * size * count * width,
    )
    own_far, own_near = (
        lax.all_to_all(x, "wide", split_axis=0, concat_axis=0, tiled=True).reshape(size, -1)
        for x in own_halves[::-1]
    )
    (near_out,) = call(
        functools.partial(select_kernel, experts, block, capacity),
        [((experts, block, sum(nears)), BF16)],
        shards,
        "v" * (groups - 1),
        "a",
        scratch=[
            *(((experts, block, near), BF16) for near in nears),
            pltpu.SemaphoreType.DMA((groups - 1,)),
        ],
        flops=SELECT_WEIGHT * 2 * size * count * sum(nears),
        vmem=24,
    )
    near_out, far_sent = lax.optimization_barrier((near_out, own_far))
    far_rows = [
        from_behind(far_sent, step) for step, near in enumerate(nears, 1) if near < width
    ]
    near_rows = lax.all_to_all(near_out, "wide", split_axis=0, concat_axis=0, tiled=True)

    total = groups * size
    slope_own, gates_own, sums_own = call(
        functools.partial(own_expert_kernel, experts, groups, block, capacity),
        [((size, hidden), BF16), ((size, 2 * devices), BF16), ((2 * devices, hidden), F32)],
        (own_near, own_far, up),
        "vvv",
        flops=2 * size * width * hidden,
        vmem=64,
    )
    pre, gates, sums, partial = call(
        functools.partial(expert_kernel, experts, groups, block, capacity, nears),
        [
            ((total - size, hidden), BF16),
            ((total - size, 2 * devices), BF16),
            ((2 * devices, hidden), F32),
            ((devices, 2, width), BF16),
        ],
        (near_rows, *far_rows, up, down, sums_own),
        "a" * (4 + len(far_rows)),
        "aaaa",
        scratch=[
            ((devices, 2, width), BF16),
            ((width, hidden), BF16),
            ((hidden, width), BF16),
            ((total - size, hidden), BF16),
            ((total - size, 2 * devices), BF16),
            ((2 * devices, hidden), F32),
            *(((experts, block, near), BF16) for near in nears),
            *(((size, width - near), BF16) for near in nears if near < width),
            pltpu.SemaphoreType.DMA((5 + 4 * (groups - 1),)),
        ],
        flops=2 * (total - size) * width * hidden,
    )
    axes = ("wide", "narrow")
    parts = lax.all_to_all(partial, axes, split_axis=0, concat_axis=0, tiled=True)
    (slope,) = call(
        slope_kernel,
        [((total - size, hidden), BF16)],
        (pre,),
        "a",
        "a",
        scratch=[
            ((total - size, hidden), BF16),
            ((total - size, hidden), BF16),
            pltpu.SemaphoreType.DMA((2, 2 * (groups - 1))),
        ],
        flops=total * hidden * 400,
    )
    parts, slope = lax.optimization_barrier((parts, slope))
    (pooled,) = call(pool_kernel, [((devices, 2, width), BF16)], (parts, own_sum), "vv", vmem=8)
    own_near, near_rows, pooled = lax.optimization_barrier((own_near, near_rows, pooled))
    pooled = lax.all_to_all(pooled, axes, split_axis=0, concat_axis=0, tiled=True)
    sources = (own_near, own_far, near_rows, *far_rows)
    (turned,) = call(
        functools.partial(turn_kernel, nears),
        [((width, total), BF16)],
        sources,
        "a" * len(sources),
        "a",
        scratch=[
            *((x.shape, BF16) for x in sources),
            ((width, total), BF16),
            pltpu.SemaphoreType.DMA((len(sources) + groups // 2,)),
        ],
        flops=total * hidden * 400,
        vmem=64,
    )
    up_grad, down_grad = call(
        backward_kernel,
        [((width, hidden), F32), ((hidden, width), F32)],
        (
            pooled, positive.reshape(1, devices), gates_own, gates, sums, down,
            turned, slope_own, slope,
        ),
        "aaaaaaaaa",
        "aa",
        scratch=[
            ((devices, 2, width), BF16),
            ((1, devices), jnp.int32),
            ((total, 2 * devices), BF16),
            ((2 * devices, hidden), F32),
            ((hidden, width), BF16),
            ((width, total), BF16),
            ((total, hidden), BF16),
            ((total, hidden), BF16),
            ((width, hidden), F32),
            ((hidden, width), F32),
            pltpu.SemaphoreType.DMA((10 + hidden // column_tile(hidden),)),
        ],
        flops=2 * total * width * hidden,
    )
    return (up_grad[None], down_grad[None])


def solution(mesh):
    return jax.shard_map(
        body,
        mesh=mesh,
        in_specs=(
            P(("wide", "narrow"), None, None, None),
            P(("wide", "narrow"), None, None),
            P(),
            P(),
            P(),
            P(),
            P("wide", None, "narrow"),
            P("wide", "narrow", None),
        ),
        out_specs=(P("wide", None, "narrow"), P("wide", "narrow", None)),
        check_vma=False,
    )
```

time: 570 us -> 107 us (0.19); the launches traced: 563 us -> 107 us
  waiting for transfers between devices: 325 us -> 38 us
  blocking collectives: 101 us -> 0 us
  local copies, waits for them, and re-layouts: 57.1 us -> 0.01 us
  matrix products: 48.8 us -> 0 us
  Pallas kernels: 0 us -> 38.5 us
  starting transfers between devices: 4.2 us -> 29.2 us
  between operations: 14.5 us -> 0.89 us
  other arithmetic: 12.4 us -> 0 us
    all_gather x2 -> x0, waiting for transfers between devices: 132 us -> none  [the longest x1 66.4 us: body(): lax.all_gather(arrived_grad, 'narrow', axis=0, tiled=True)]
    unnamed x5 -> x0, waiting for transfers between devices: 118 us -> none
    all_gather x1 -> x0, blocking collectives: 66 us -> none  [body(): lax.all_gather(passage_unit_vector, ('wide', 'narrow'), axis=0, tiled=True)]
    reduce_scatter x1 -> x0, waiting for transfers between devices: 62.1 us -> none  [body(): lax.psum_scatter(partial_value.astype(jnp.bfloat16), 'narrow', scatter_di...]
    dot_general x11 -> x0, matrix products: 48.8 us -> none  [the longest x2 25 us: contract_rows(): lax.dot_general(left, right, (((0,), (0,)), ((), ())), preferred_element_...]
    pallas_call x0 -> x9, Pallas kernels: none -> 38.5 us  [call(): pl.pallas_call(kernel, out_shape=outs, in_specs=[pl.BlockSpec(memory_spac...]
    all_to_all x2 -> x0, blocking collectives: 35.1 us -> none  [the longest x1 18.6 us: body(): lax.all_to_all(outgoing, 'wide', split_axis=0, concat_axis=0, tiled=True)]
    ppermute x0 -> x5, waiting for transfers between devices: none -> 24.2 us  [from_behind(): lax.ppermute(array, 'narrow', [(i, (i + step) % groups) for i in range(gr...]
  transfers between devices with their start and end apart: 5 -> 10, of which waited for: 5 -> 7; matrix products, arithmetic and copies ran while one was open for 0% -> 0% of each run, Pallas kernels for 0% -> 17%
where the time goes in v1:
time: 107 us
  Pallas kernels  38.5 us (36%)
  waiting for transfers between devices  38 us (36%)
  starting transfers between devices  29.2 us (27%)
    pallas_call x9, Pallas kernels, call(): pl.pallas_call(kernel, out_shape=outs, in_specs=[pl.BlockSpec(memory_spac...  38.5 us
    ppermute x5, waiting for transfers between devices, from_behind(): lax.ppermute(array, 'narrow', [(i, (i + step) % groups) for i in range(gr...  24.2 us
    ppermute x5, starting transfers between devices, from_behind(): lax.ppermute(array, 'narrow', [(i, (i + step) % groups) for i in range(gr...  9.07 us
    all_to_all x2, starting transfers between devices, body(): lax.all_to_all(x, 'wide', split_axis=0, concat_axis=0, tiled=True)  8.24 us
    all_to_all x2, waiting for transfers between devices, body(): lax.all_to_all(x, 'wide', split_axis=0, concat_axis=0, tiled=True)  7.55 us
    all_to_all x1, starting transfers between devices, body(): lax.all_to_all(partial, axes, split_axis=0, concat_axis=0, tiled=True)  4.34 us
    all_to_all x1, starting transfers between devices, body(): lax.all_to_all(near_out, 'wide', split_axis=0, concat_axis=0, tiled=True)  4.32 us
    all_to_all x1, waiting for transfers between devices, body(): lax.all_to_all(pooled, axes, split_axis=0, concat_axis=0, tiled=True)  3.27 us
  transfers between devices with their start and end apart: 10, of which 7 were waited for; matrix products, arithmetic and copies ran while one was open for 0% of the time, Pallas kernels for 17%

profile of v1, /device:TPU:0, one launch (start us, length us, event | category | flops | bytes accessed | tf_op | source)
XLA Modules:
  0.0 106.5 jit_solution(11666959434697192916)
XLA Ops:
  0.6 6.1 %shard_map.95 = (bf16[264,384]{1,0:T(8,128)(2,1)}, bf16[264,768]{1,0:T(8,128)(2,1)}, f32[2,768]{1,0:T(2,128)}) custom-call(bf16[256,768]{1,0:T(8,128)(2,1)} %bitcast.16, s32[2,256]{1,0:T(2,128)} %bitcast.18, bf16[8,768]{1,0:T(8,128)(2,1)} %bitcast.17, bf16[768,2304]{1,0:T(8,128)(2,1)} %qkv_hbm.1, bf16[768,768]{1,0:T(8,128)(2,1)} %out_hbm.1), custom_call_target="tpu_custom_call" | custom-call | flops 1509949440 | bytes 5740544 | tf_op jit(solution)/shard_map/pallas_call | solution.py:494
  6.7 4.1 %collective-permute-start.1 = (bf16[264,768]{1,0:T(8,128)(2,1)}, bf16[264,768]{1,0:T(8,128)(2,1)S(1)}, u32[]{:S(2)}, u32[]{:S(2)}) collective-permute-start(bf16[264,768]{1,0:T(8,128)(2,1)} %get-tuple-element.23.payload_ref), channel_id=1, source_target_pairs={{0,2},{1,3},{2,0},{3,1},{4,6},{5,7},{6,4},{7,5},{8,10},{9,11},{10,... | collective-permute-start | bytes 1216520 | tf_op jit(solution)/shard_map/ppermute | solution.py:521
  10.8 2.4 %shard_map.96 = (bf16[8,72,384]{2,1,0:T(8,128)(2,1)}, bf16[8,72,384]{2,1,0:T(8,128)(2,1)}) custom-call(bf16[264,768]{1,0:T(8,128)(2,1)} %get-tuple-element.23.payload_ref), custom_call_target="tpu_custom_call" | custom-call | flops 226492416 | bytes 1290240 | tf_op jit(solution)/shard_map/pallas_call | solution.py:494
  13.2 4.1 %all-to-all-start.1 = ((bf16[8,72,384]{2,1,0:T(8,128)(2,1)}), bf16[8,72,384]{2,1,0:T(8,128)(2,1)}, u32[]{:S(2)}, u32[]{:S(2)}) async-start(bf16[8,72,384]{2,1,0:T(8,128)(2,1)} %get-tuple-element.26), calls=%async_computation.1 | async-start | bytes 884736 | tf_op jit(solution)/shard_map/all_to_all | solution.py:551
  17.3 1.4 %collective-permute-start.2 = (bf16[264,384]{1,0:T(8,128)(2,1)}, bf16[264,384]{1,0:T(8,128)(2,1)S(1)}, u32[]{:S(2)}, u32[]{:S(2)}) collective-permute-start(bf16[264,384]{1,0:T(8,128)(2,1)} %get-tuple-element.25), channel_id=1, source_target_pairs={{0,3},{1,0},{2,1},{3,2},{4,7},{5,4},{6,5},{7,6},{8,11},{9,8},{10,9... | collective-permute-start | bytes 608264 | tf_op jit(solution)/shard_map/ppermute | solution.py:521
  18.7 0.7 collective-permute-start
  19.4 6.8 %all-to-all-done.1 = bf16[8,72,384]{2,1,0:T(8,128)(2,1)} async-done(((bf16[8,72,384]{2,1,0:T(8,128)(2,1)}), bf16[8,72,384]{2,1,0:T(8,128)(2,1)}, u32[]{:S(2)}, u32[]{:S(2)}) %all-to-all-start.1) | async-done | bytes 442400 | tf_op jit(solution)/shard_map/all_to_all | solution.py:551
  26.2 4.1 %all-to-all-start = ((bf16[8,72,384]{2,1,0:T(8,128)(2,1)}), bf16[8,72,384]{2,1,0:T(8,128)(2,1)}, u32[]{:S(2)}, u32[]{:S(2)}) async-start(bf16[8,72,384]{2,1,0:T(8,128)(2,1)} %get-tuple-element.24), calls=%async_computation | async-start | bytes 884736 | tf_op jit(solution)/shard_map/all_to_all | solution.py:551
  30.3 6.4 %collective-permute-done.2.refs_2_ = bf16[264,384]{1,0:T(8,128)(2,1)S(1)} collective-permute-done((bf16[264,384]{1,0:T(8,128)(2,1)}, bf16[264,384]{1,0:T(8,128)(2,1)S(1)}, u32[]{:S(2)}, u32[]{:S(2)}) %collective-permute-start.2) | collective-permute-done | bytes 202784 | tf_op jit(solution)/shard_map/ppermute | solution.py:521
  36.7 0.0 collective-permute-done.refs_0_
  36.7 0.0 collective-permute-done.1.refs_1_
  36.7 1.7 %shard_map.97 = bf16[8,72,1536]{2,1,0:T(8,128)(2,1)} custom-call(bf16[264,384]{1,0:T(8,128)(2,1)S(1)} %collective-permute-done.refs_0_, bf16[264,768]{1,0:T(8,128)(2,1)S(1)} %collective-permute-done.1.refs_1_, bf16[264,384]{1,0:T(8,128)(2,1)S(1)} %collective-permute-done.2.refs_2_), custom_call_target="tpu_custom_call" | custom-call | flops 452984832000 | bytes 2580480 | tf_op jit(solution)/shard_map/pallas_call | solution.py:494
  38.4 0.8 all-to-all-done
  39.2 4.3 %all-to-all-start.2 = ((bf16[8,72,1536]{2,1,0:T(8,128)(2,1)}), bf16[8,72,1536]{2,1,0:T(8,128)(2,1)}, u32[]{:S(2)}, u32[]{:S(2)}) async-start(bf16[8,72,1536]{2,1,0:T(8,128)(2,1)} %shard_map.97), calls=%async_computation.2 | async-start | bytes 3538944 | tf_op jit(solution)/shard_map/all_to_all | solution.py:571
  43.5 2.9 %collective-permute-start.4 = (bf16[576,384]{1,0:T(8,128)(2,1)}, bf16[576,384]{1,0:T(8,128)(2,1)}, u32[]{:S(2)}, u32[]{:S(2)}) collective-permute-start(bf16[576,384]{1,0:T(8,128)(2,1)} %bitcast.5.far_ref.refs_1_), channel_id=1, source_target_pairs={{0,3},{1,0},{2,1},{3,2},{4,7},{5,4},{6,5},{7,6},{8,11},{9,8},{10,9... | collective-permute-start | bytes 1327112 | tf_op jit(solution)/shard_map/ppermute | solution.py:521
  46.4 0.0 collective-permute-start.3
  46.4 4.0 %shard_map.98 = (bf16[576,768]{1,0:T(8,128)(2,1)}, bf16[576,64]{1,0:T(8,128)(2,1)}, f32[64,768]{1,0:T(8,128)}) custom-call(bf16[576,384]{1,0:T(8,128)(2,1)} %bitcast.4.near_ref.refs_0_, bf16[576,384]{1,0:T(8,128)(2,1)} %bitcast.5.far_ref.refs_1_, bf16[768,768]{1,0:T(8,128)(2,1)} %bitcast.12), custom_call_target="tpu_custom_call" | custom-call | flops 679477248 | bytes 3219456 | tf_op jit(solution)/shard_map/pallas_call | solution.py:494
  50.4 6.8 %collective-permute-done.4.refs_2_.refs_4_ = bf16[576,384]{1,0:T(8,128)(2,1)} collective-permute-done((bf16[576,384]{1,0:T(8,128)(2,1)}, bf16[576,384]{1,0:T(8,128)(2,1)}, u32[]{:S(2)}, u32[]{:S(2)}) %collective-permute-start.4) | collective-permute-done | bytes 442400 | tf_op jit(solution)/shard_map/ppermute | solution.py:521
  57.3 11.0 %collective-permute-done.3.refs_1_.refs_3_ = bf16[576,384]{1,0:T(8,128)(2,1)} collective-permute-done((bf16[576,384]{1,0:T(8,128)(2,1)}, bf16[576,384]{1,0:T(8,128)(2,1)}, u32[]{:S(2)}, u32[]{:S(2)}) %collective-permute-start.3) | collective-permute-done | bytes 442400 | tf_op jit(solution)/shard_map/ppermute | solution.py:521
  68.2 0.0 all-to-all-done.2.refs_0_.refs_2_
  68.2 6.2 %shard_map.99 = (bf16[1728,768]{1,0:T(8,128)(2,1)}, bf16[1728,64]{1,0:T(8,128)(2,1)}, f32[64,768]{1,0:T(8,128)}, bf16[32,2,768]{2,1,0:T(2,128)(2,1)}) custom-call(bf16[8,72,1536]{2,1,0:T(8,128)(2,1)} %all-to-all-done.2.refs_0_.refs_2_, bf16[576,384]{1,0:T(8,128)(2,1)} %collective-permute-done.3.refs_1_.refs_3_, ...), custom_call_target="tpu_custom_call" | custom-call | flops 2038431744 | bytes 8380416 | tf_op jit(solution)/shard_map/pallas_call | solution.py:494
  74.4 4.3 %all-to-all-start.3 = ((bf16[32,2,768]{2,1,0:T(2,128)(2,1)}), bf16[32,2,768]{2,1,0:T(2,128)(2,1)S(1)}, u32[]{:S(2)}, u32[]{:S(2)}) async-start(bf16[32,2,768]{2,1,0:T(2,128)(2,1)} %get-tuple-element.30), calls=%async_computation.3 | async-start | bytes 196608 | tf_op jit(solution)/shard_map/all_to_all | solution.py:607
  78.7 0.0 copy-start
  78.8 4.8 %shard_map.100.slope_hbm = bf16[1728,768]{1,0:T(8,128)(2,1)} custom-call(bf16[1728,768]{1,0:T(8,128)(2,1)} %get-tuple-element.31.pre_hbm), custom_call_target="tpu_custom_call" | custom-call | flops 707788800 | bytes 5308416 | tf_op jit(solution)/shard_map/pallas_call | solution.py:494
  83.5 3.0 %all-to-all-done.3.parts_ref = bf16[32,2,768]{2,1,0:T(2,128)(2,1)S(1)} async-done(((bf16[32,2,768]{2,1,0:T(2,128)(2,1)}), bf16[32,2,768]{2,1,0:T(2,128)(2,1)S(1)}, u32[]{:S(2)}, u32[]{:S(2)}) %all-to-all-start.3) | async-done | bytes 98336 | tf_op jit(solution)/shard_map/all_to_all | solution.py:607
  86.5 0.0 copy-done
  86.5 0.8 shard_map.101
  87.3 3.3 %all-to-all-start.4 = ((bf16[32,2,768]{2,1,0:T(2,128)(2,1)}), bf16[32,2,768]{2,1,0:T(2,128)(2,1)}, u32[]{:S(2)}, u32[]{:S(2)}) async-start(bf16[32,2,768]{2,1,0:T(2,128)(2,1)} %shard_map.101), calls=%async_computation.4 | async-start | bytes 196608 | tf_op jit(solution)/shard_map/all_to_all | solution.py:624
  90.5 4.7 %shard_map.102.turned_hbm = bf16[768,2304]{1,0:T(8,128)(2,1)} custom-call(bf16[576,384]{1,0:T(8,128)(2,1)} %bitcast.4.near_ref.refs_0_, bf16[576,384]{1,0:T(8,128)(2,1)} %bitcast.5.far_ref.refs_1_, bf16[8,72,1536]{2,1,0:T(8,128)(2,1)} %all-to-all-done.2.refs_0_.refs_2_, bf16[576,384]{1,0:T(8,128)(2,1)} %collective-permute-done.3.refs_1_.refs_3_, ...), custom_call_target="tpu_custom_call" | custom-call | flops 707788800 | bytes 7077888 | tf_op jit(solution)/shard_map/pallas_call | solution.py:494
  95.2 3.3 %all-to-all-done.4.pooled_hbm = bf16[32,2,768]{2,1,0:T(2,128)(2,1)} async-done(((bf16[32,2,768]{2,1,0:T(2,128)(2,1)}), bf16[32,2,768]{2,1,0:T(2,128)(2,1)}, u32[]{:S(2)}, u32[]{:S(2)}) %all-to-all-start.4) | async-done | bytes 98336 | tf_op jit(solution)/shard_map/all_to_all | solution.py:624
  98.5 7.9 %shard_map.103 = (f32[768,768]{1,0:T(8,128)}, f32[768,768]{1,0:T(8,128)}) custom-call(bf16[32,2,768]{2,1,0:T(2,128)(2,1)} %all-to-all-done.4.pooled_hbm, s32[1,32]{1,0:T(1,128)} %bitcast.19, bf16[576,64]{1,0:T(8,128)(2,1)} %get-tuple-element.35.gates_own_hbm, bf16[1728,64]{1,0:T(8,128)(2,1)} %get-tuple-element.36.gates_hbm, ...), custom_call_target="tpu_custom_call" | custom-call | flops 2717908992 | bytes 13566080 | tf_op jit(solution)/shard_map/pallas_call | solution.py:494
Async XLA Ops:
  6.7 30.0 %collective-permute-start.1 = (bf16[264,768]{1,0:T(8,128)(2,1)}, bf16[264,768]{1,0:T(8,128)(2,1)S(1)}, u32[]{:S(2)}, u32[]{:S(2)}) collective-permute-start(bf16[264,768]{1,0:T(8,128)(2,1)} %get-tuple-element.23.payload_ref), channel_id=1, source_target_pairs={{0,2},{1,3},{2,0},{3,1},{4,6},{5,7},{6,4},{7,5},{8,10},{9,11},{10,... | collective-permute-start | bytes 1216520 | tf_op jit(solution)/shard_map/ppermute | solution.py:521
  13.2 13.0 %all-to-all-start.1 = ((bf16[8,72,384]{2,1,0:T(8,128)(2,1)}), bf16[8,72,384]{2,1,0:T(8,128)(2,1)}, u32[]{:S(2)}, u32[]{:S(2)}) async-start(bf16[8,72,384]{2,1,0:T(8,128)(2,1)} %get-tuple-element.26), calls=%async_computation.1 | async-start | bytes 884736 | tf_op jit(solution)/shard_map/all_to_all | solution.py:551
  17.3 19.4 %collective-permute-start.2 = (bf16[264,384]{1,0:T(8,128)(2,1)}, bf16[264,384]{1,0:T(8,128)(2,1)S(1)}, u32[]{:S(2)}, u32[]{:S(2)}) collective-permute-start(bf16[264,384]{1,0:T(8,128)(2,1)} %get-tuple-element.25), channel_id=1, source_target_pairs={{0,3},{1,0},{2,1},{3,2},{4,7},{5,4},{6,5},{7,6},{8,11},{9,8},{10,9... | collective-permute-start | bytes 608264 | tf_op jit(solution)/shard_map/ppermute | solution.py:521
  18.7 18.0 %collective-permute-start = (bf16[264,384]{1,0:T(8,128)(2,1)}, bf16[264,384]{1,0:T(8,128)(2,1)S(1)}, u32[]{:S(2)}, u32[]{:S(2)}) collective-permute-start(bf16[264,384]{1,0:T(8,128)(2,1)} %get-tuple-element.25), channel_id=1, source_target_pairs={{0,1},{1,2},{2,3},{3,0},{4,5},{5,6},{6,7},{7,4},{8,9},{9,10},{10,1... | collective-permute-start | bytes 608264 | tf_op jit(solution)/shard_map/ppermute | solution.py:521
  26.2 13.0 %all-to-all-start = ((bf16[8,72,384]{2,1,0:T(8,128)(2,1)}), bf16[8,72,384]{2,1,0:T(8,128)(2,1)}, u32[]{:S(2)}, u32[]{:S(2)}) async-start(bf16[8,72,384]{2,1,0:T(8,128)(2,1)} %get-tuple-element.24), calls=%async_computation | async-start | bytes 884736 | tf_op jit(solution)/shard_map/all_to_all | solution.py:551
  39.2 29.0 %all-to-all-start.2 = ((bf16[8,72,1536]{2,1,0:T(8,128)(2,1)}), bf16[8,72,1536]{2,1,0:T(8,128)(2,1)}, u32[]{:S(2)}, u32[]{:S(2)}) async-start(bf16[8,72,1536]{2,1,0:T(8,128)(2,1)} %shard_map.97), calls=%async_computation.2 | async-start | bytes 3538944 | tf_op jit(solution)/shard_map/all_to_all | solution.py:571
  43.5 13.8 %collective-permute-start.4 = (bf16[576,384]{1,0:T(8,128)(2,1)}, bf16[576,384]{1,0:T(8,128)(2,1)}, u32[]{:S(2)}, u32[]{:S(2)}) collective-permute-start(bf16[576,384]{1,0:T(8,128)(2,1)} %bitcast.5.far_ref.refs_1_), channel_id=1, source_target_pairs={{0,3},{1,0},{2,1},{3,2},{4,7},{5,4},{6,5},{7,6},{8,11},{9,8},{10,9... | collective-permute-start | bytes 1327112 | tf_op jit(solution)/shard_map/ppermute | solution.py:521
  46.4 21.8 %collective-permute-start.3 = (bf16[576,384]{1,0:T(8,128)(2,1)}, bf16[576,384]{1,0:T(8,128)(2,1)}, u32[]{:S(2)}, u32[]{:S(2)}) collective-permute-start(bf16[576,384]{1,0:T(8,128)(2,1)} %bitcast.5.far_ref.refs_1_), channel_id=1, source_target_pairs={{0,1},{1,2},{2,3},{3,0},{4,5},{5,6},{6,7},{7,4},{8,9},{9,10},{10,1... | collective-permute-start | bytes 1327112 | tf_op jit(solution)/shard_map/ppermute | solution.py:521
  74.4 12.1 %all-to-all-start.3 = ((bf16[32,2,768]{2,1,0:T(2,128)(2,1)}), bf16[32,2,768]{2,1,0:T(2,128)(2,1)S(1)}, u32[]{:S(2)}, u32[]{:S(2)}) async-start(bf16[32,2,768]{2,1,0:T(2,128)(2,1)} %get-tuple-element.30), calls=%async_computation.3 | async-start | bytes 196608 | tf_op jit(solution)/shard_map/all_to_all | solution.py:607
  78.7 7.8 %copy-start = (f32[2,768]{1,0:T(2,128)S(1)}, f32[2,768]{1,0:T(2,128)}, u32[]{:S(2)}) copy-start(f32[2,768]{1,0:T(2,128)} %get-tuple-element.33.own_ref) | copy-start | bytes 18436
  87.3 11.2 %all-to-all-start.4 = ((bf16[32,2,768]{2,1,0:T(2,128)(2,1)}), bf16[32,2,768]{2,1,0:T(2,128)(2,1)}, u32[]{:S(2)}, u32[]{:S(2)}) async-start(bf16[32,2,768]{2,1,0:T(2,128)(2,1)} %shard_map.101), calls=%async_computation.4 | async-start | bytes 196608 | tf_op jit(solution)/shard_map/all_to_all | solution.py:624
